TPU v7x, 32 devices: a whole 2x2x4 slice. The times are simulated.
32 devices in a mesh: dom: 8 (over y, x, core), rep: 4 (over z).
Axes of the slice: x: 2, y: 2, z: 4, core: 2. Of those that a mesh axis runs over, the one named last changes fastest.
Arguments:
- features: float32 [2048, 256], P('dom'), may hold values from -6 to 6
- tile_values: bfloat16 [8, 64, 128, 128], P('dom', 'rep'), may hold values from 0 to 0.03125
- tile_rows: int32 [8, 64], P('dom', 'rep'), may hold values from 0 to 1
- tile_cols: int32 [8, 64], P('dom', 'rep'), may hold values from 0 to 15, as said below
- weight: float32 [256, 256], replicated, may hold values from -0.375 to 0.375
- bias: float32 [256], replicated, may hold values from -3 to 3
- cotangent: float32 [2048, 256], P('dom'), may hold values from -6 to 6
Outputs:
- activations: float32 [2048, 256], P('dom')
- grad_features: float32 [2048, 256], P('dom')
- grad_weight: float32 [256, 256], replicated
- grad_bias: float32 [256], replicated
Inputs may be any that keep to these rules, and one draw needn't show every extreme that they name: `tile_cols`: within each share of 16 consecutive tiles of a partition, every tile column 0 to 15 appears exactly once.
All inputs are finite; a program needn't handle non-finite values.
Results may differ from a plain program's by a relative error of at most 0.0003.
Values sent between devices are 32-bit elements; how exact they have to be, the bound alone decides.
A program may use at most 64 MiB of HBM per device.

v0:
```python
import jax
import jax.numpy as jnp
from jax import lax
from jax.sharding import PartitionSpec as P


def body(features, tile_values, tile_rows, tile_cols, weight, bias, cotangent):
    highest = lax.Precision.HIGHEST
    values = tile_values[0].astype(jnp.float32)
    row_ids = tile_rows[0]
    col_ids = tile_cols[0]
    tile_size = values.shape[1]
    node_rows = features.shape[0]
    feat_width = features.shape[1]
    row_blocks = node_rows // tile_size
    shard_piece = lax.all_gather(features, "dom", axis=0, tiled=True)
    block_count = shard_piece.shape[0] // tile_size
    blocks = shard_piece.reshape(block_count, tile_size, feat_width)
    offsets = col_ids[:, None]
    select = (offsets == jnp.arange(block_count, dtype=jnp.int32)[None, :]).astype(jnp.float32)
    selected = jnp.einsum("sn,nif->sif", select, blocks, precision=highest)
    products = jnp.einsum("sij,sjf->sif", values, selected, precision=highest)
    row_select = (row_ids[None, :] == jnp.arange(row_blocks, dtype=jnp.int32)[:, None]).astype(
        jnp.float32
    )
    partial_rows = jnp.einsum("bs,sif->bif", row_select, products, precision=highest).reshape(
        node_rows, feat_width
    )
    aggregated = lax.psum(partial_rows, "rep")
    before = jnp.dot(aggregated, weight, precision=highest) + bias
    gate_value = jax.nn.sigmoid(before)
    output = before * gate_value
    grad_pre = cotangent * gate_value * (1.0 + before * (1.0 - gate_value))
    messages = jnp.dot(grad_pre, weight.T, precision=highest)
    weight_term = jnp.dot(aggregated.T, grad_pre, precision=highest)
    activations, messages, weight_term, bias_term = (
        output,
        messages,
        weight_term,
        jnp.sum(grad_pre, axis=0),
    )
    grad_weight, grad_bias = lax.psum((weight_term, bias_term), "dom")
    message_blocks = messages.reshape(row_blocks, tile_size, feat_width)
    picked_messages = jnp.einsum("bs,bif->sif", row_select, message_blocks, precision=highest)
    returned = jnp.einsum("sji,sjf->sif", values, picked_messages, precision=highest)
    block_count = node_rows * lax.axis_size("dom") // tile_size
    offsets = col_ids[None, :]
    select = (offsets == jnp.arange(block_count, dtype=jnp.int32)[:, None]).astype(jnp.float32)
    source_part = lax.psum_scatter(
        jnp.einsum("ns,sif->nif", select, returned, precision=highest).reshape(
            node_rows * lax.axis_size("dom"), feat_width
        ),
        "dom",
        scatter_dimension=0,
        tiled=True,
    )
    grad_features = lax.psum(source_part, "rep")
    return (activations, grad_features, grad_weight, grad_bias)


def solution(mesh):
    return jax.shard_map(
        body,
        mesh=mesh,
        in_specs=(
            P("dom", None),
            P("dom", "rep", None, None),
            P("dom", "rep"),
            P("dom", "rep"),
            P(),
            P(),
            P("dom", None),
        ),
        out_specs=(P("dom", None), P("dom", None), P(), P()),
        check_vma=False,
    )
```

profile of v0, /device:TPU:0, one launch (start us, length us, event | category | flops | bytes accessed | tf_op | source)
XLA Modules:
  0.0 246.7 jit_solution(1948898299063535947)
XLA Ops:
  7.2 0.0 copy-start
  7.2 0.0 all-gather.2.cloned.1.call-start
  7.2 0.7 all-gather.2.cloned.1.call-update
  7.9 0.0 all-reduce.4.cloned.1.call-start
  8.0 32.6 %all-gather.2.cloned.1.call-done = f32[2048,256]{1,0:T(8,128)} async-done(((f32[256,256]{1,0:T(8,128)}), f32[2048,256]{1,0:T(8,128)}) %all-gather.2.cloned.1.call-update) | async-done | bytes 2097168 | tf_op jit(solution)/shard_map/all_gather | solution.py:16
  40.5 3.9 %fusion.8 = f32[16,128,256]{2,0,1:T(8,128)S(1)} fusion(f32[16,128,256]{2,1,0:T(8,128)} %bitcast.35, s32[16]{0:T(128)} %bitcast.40), kind=kOutput, calls=%fused_computation.8 | convolution fusion | flops 100663552 | bytes 4194368 | tf_op jit(solution)/shard_map/sn,nif->sif/dot_general | solution.py:21
  44.5 0.0 copy-done
  44.5 4.1 %fusion.6 = f32[16,256,128]{2,1,0:T(8,128)} fusion(f32[16,128,256]{2,0,1:T(8,128)S(1)} %fusion.8, bf16[1,16,128,128]{3,2,1,0:T(8,128)(2,1)S(1)} %copy-done), kind=kOutput, calls=%fused_computation.6 | convolution fusion | flops 805306368 | bytes 4718592 | tf_op jit(solution)/shard_map/sij,sjf->sif/dot_general | solution.py:22
  48.5 0.0 copy-start.3
  48.5 2.2 copy.15
  50.8 0.0 copy-start.1
  50.8 0.0 copy-start.5
  50.8 0.0 copy-start.6
  50.8 0.0 copy-done.3
  50.8 0.8 fusion.2
  51.6 0.7 copy.11
  52.4 0.0 all-reduce.4.cloned.1.call-update
  52.4 0.2 reduce-scatter.2.cloned.1.call-start
  52.6 35.2 %all-reduce.4.cloned.1.call-done = f32[256,256]{1,0:T(8,128)} async-done(((f32[256,256]{1,0:T(8,128)}), f32[256,256]{1,0:T(8,128)}) %all-reduce.4.cloned.1.call-update) | async-done | bytes 262160 | tf_op jit(solution)/shard_map/psum | solution.py:29
  87.9 0.0 copy-done.1
  87.9 0.0 copy-done.5
  87.9 0.0 copy-done.6
  87.9 2.1 fusion.25
  90.0 0.4 fusion.26
  90.4 1.1 fusion.12
  91.5 2.7 %fusion.4 = f32[16,256,128]{2,1,0:T(8,128)S(1)} fusion(f32[16,128,256]{2,0,1:T(8,128)S(1)} %fusion.12, bf16[1,16,128,128]{3,2,1,0:T(8,128)(2,1)S(1)} %copy-done), kind=kOutput, calls=%fused_computation.4 | convolution fusion | flops 805306368 | bytes 4718592 | tf_op jit(solution)/shard_map/sji,sjf->sif/dot_general | solution.py:45
  94.3 0.0 copy-start.4
  94.3 2.1 copy.18
  96.4 0.0 copy-done.4
  96.4 2.7 %fusion = f32[16,128,256]{2,0,1:T(8,128)S(1)} fusion(f32[16,256,128]{1,0,2:T(8,128)} %copy.18, s32[16]{0:T(128)S(1)} %bitcast.41), kind=kOutput, calls=%fused_computation | convolution fusion | flops 100663552 | bytes 4194368 | tf_op jit(solution)/shard_map/ns,sif->nif/dot_general | solution.py:50
  99.1 2.6 %copy.12 = f32[16,128,256]{2,1,0:T(8,128)} copy(f32[16,128,256]{2,0,1:T(8,128)S(1)} %fusion) | data formatting | bytes 4194304 | tf_op jit(solution)/shard_map/ns,sif->nif/dot_general | solution.py:50
  101.6 0.0 copy-start.2
  101.6 0.0 reduce-scatter.2.cloned.1.call-update
  101.6 0.0 all-reduce.8.cloned.1.call-start
  101.7 0.9 copy-done.2
  102.6 1.3 fusion.27
  103.9 0.0 all-reduce.8.cloned.1.call-update
  103.9 0.0 all-reduce.6.cloned.1.call-start
  103.9 38.8 %reduce-scatter.2.cloned.1.call-done = f32[256,256]{1,0:T(8,128)} async-done(((f32[2048,256]{1,0:T(8,128)}), f32[256,256]{1,0:T(8,128)}) %reduce-scatter.2.cloned.1.call-update) | async-done | bytes 262160 | tf_op jit(solution)/shard_map/reduce_scatter | solution.py:49
  142.8 0.0 all-reduce.6.cloned.1.call-update
  142.8 13.2 %psum.31 = f32[256]{0:T(256)} all-reduce(f32[256]{0:T(256)S(1)} %get-tuple-element.4), channel_id=1, replica_groups=mesh['dom'=8,'rep'=4] {'dom'}, use_global_device_ids=true, to_apply=%region_5.0 | all-reduce | flops 256 | bytes 2048 | tf_op jit(solution)/shard_map/psum | solution.py:42
  156.0 43.8 %all-reduce.8.cloned.1.call-done = f32[256,256]{1,0:T(8,128)} async-done(((f32[256,256]{1,0:T(8,128)}), f32[256,256]{1,0:T(8,128)}) %all-reduce.8.cloned.1.call-update) | async-done | bytes 262160 | tf_op jit(solution)/shard_map/psum | solution.py:42
  199.8 37.0 %all-reduce.6.cloned.1.call-done = f32[256,256]{1,0:T(8,128)} async-done(((f32[256,256]{1,0:T(8,128)}), f32[256,256]{1,0:T(8,128)}) %all-reduce.6.cloned.1.call-update) | async-done | bytes 262160 | tf_op jit(solution)/shard_map/psum | solution.py:57
  236.8 1.7 copy.30
  238.5 1.7 copy.31
Async XLA Ops:
  7.2 37.3 %copy-start = (bf16[1,16,128,128]{3,2,1,0:T(8,128)(2,1)S(1)}, bf16[1,16,128,128]{3,2,1,0:T(8,128)(2,1)}, u32[]{:S(2)}) copy-start(bf16[1,16,128,128]{3,2,1,0:T(8,128)(2,1)} %param.8) | copy-start | bytes 1572868
  7.2 33.4 %all-gather.2.cloned.1.call-start = ((), (), s32[]{:S(2)}) async-start(), calls=%async_computation.1 | async-start | bytes 2359296 | tf_op jit(solution)/shard_map/all_gather | solution.py:16
  7.9 79.9 %all-reduce.4.cloned.1.call-start = ((), (), s32[]{:S(2)}) async-start(), calls=%async_computation.2 | async-start | bytes 524288 | tf_op jit(solution)/shard_map/psum | solution.py:29
  48.5 2.3 copy-start.3
  50.8 37.1 %copy-start.1 = (f32[256,256]{1,0:T(8,128)S(1)}, f32[256,256]{1,0:T(8,128)}, u32[]{:S(2)}) copy-start(f32[256,256]{1,0:T(8,128)} %param.11) | copy-start | bytes 786436
  50.8 37.0 %copy-start.5 = (f32[256,256]{1,0:T(8,128)S(1)}, f32[256,256]{1,0:T(8,128)}, u32[]{:S(2)}) copy-start(f32[256,256]{1,0:T(8,128)} %param.13) | copy-start | bytes 786436
  50.8 37.0 %copy-start.6 = (f32[256]{0:T(256)S(1)}, f32[256]{0:T(256)}, u32[]{:S(2)}) copy-start(f32[256]{0:T(256)} %param.12) | copy-start | bytes 3076
  52.4 90.4 %reduce-scatter.2.cloned.1.call-start = ((), (), s32[]{:S(2)}) async-start(), calls=%async_computation.3 | async-start | bytes 2359296 | tf_op jit(solution)/shard_map/reduce_scatter | solution.py:49
  94.3 2.1 copy-start.4
  101.6 0.9 copy-start.2
  101.6 98.2 %all-reduce.8.cloned.1.call-start = ((), (), s32[]{:S(2)}) async-start(), calls=%async_computation.5 | async-start | bytes 524288 | tf_op jit(solution)/shard_map/psum | solution.py:42
  103.9 132.9 %all-reduce.6.cloned.1.call-start = ((), (), s32[]{:S(2)}) async-start(), calls=%async_computation.4 | async-start | bytes 524288 | tf_op jit(solution)/shard_map/psum | solution.py:57
Sparse Core Ops, SparseCore 0:
  9.9 30.5 all-gather.1
  52.5 35.2 all-reduce.3
  101.8 40.9 reduce-scatter.1
  146.2 53.5 all-reduce.7
  202.1 34.6 all-reduce.5
where the time goes:
time: 247 us
  waiting for transfers between devices  188 us (76%)
  matrix products  19.2 us (8%)
  between operations  13.9 us (6%)
  blocking collectives  13.2 us (5%)
  local copies, waits for them, and re-layouts  11.8 us (5%)
    psum x1, waiting for transfers between devices, body(): grad_weight, grad_bias = lax.psum((weight_term, bias_term), 'dom')  43.8 us
    reduce_scatter x1, waiting for transfers between devices, body(): lax.psum_scatter(jnp.einsum('ns,sif->nif', select, returned, precision=hi...  38.8 us
    psum x1, waiting for transfers between devices, body(): grad_features = lax.psum(source_part, 'rep')  37 us
    psum x1, waiting for transfers between devices, body(): aggregated = lax.psum(partial_rows, 'rep')  35.2 us
    all_gather x1, waiting for transfers between devices, body(): shard_piece = lax.all_gather(features, 'dom', axis=0, tiled=True)  32.6 us
    psum x1, blocking collectives, body(): grad_weight, grad_bias = lax.psum((weight_term, bias_term), 'dom')  13.2 us
  transfers between devices with their start and end apart: 5, of which 5 were waited for; matrix products, arithmetic and copies ran while one was open for 1% of the time, Pallas kernels for 0%

commit v1 on v0

--- a/solution.py
+++ b/solution.py
@@ -13,7 +13,12 @@
     node_rows = features.shape[0]
     feat_width = features.shape[1]
     row_blocks = node_rows // tile_size
-    shard_piece = lax.all_gather(features, "dom", axis=0, tiled=True)
+    ring = [features]
+    for hop in range(7):
+        ring.append(lax.ppermute(ring[-1], "dom", [(dev, (dev + 1) % 8) for dev in range(8)]))
+    shard_piece = jnp.roll(
+        jnp.concatenate(ring[::-1], axis=0), (lax.axis_index("dom") + 1) * ring[0].shape[0], axis=0
+    )
     block_count = shard_piece.shape[0] // tile_size
     blocks = shard_piece.reshape(block_count, tile_size, feat_width)
     offsets = col_ids[:, None]

time: 247 us -> 263 us (1.065)
  waiting for transfers between devices: 188 us -> 204 us
    ppermute x0 -> x7, waiting for transfers between devices: none -> 47.3 us  [body(): lax.ppermute(ring[-1], 'dom', [(dev, (dev + 1) % 8) for dev in range(8)])]
    all_gather x1 -> x0, waiting for transfers between devices: 32.6 us -> none  [body(): shard_piece = lax.all_gather(features, 'dom', axis=0, tiled=True)]
  transfers between devices with their start and end apart: 5 -> 11, of which waited for: 5 -> 11; matrix products, arithmetic and copies ran while one was open for 1% -> 0% of each run, Pallas kernels for 0% -> 0%
where the time goes in v1:
time: 263 us
  waiting for transfers between devices  204 us (78%)
  matrix products  17.6 us (7%)
  between operations  14 us (5%)
  blocking collectives  13.2 us (5%)
  local copies, waits for them, and re-layouts  12.7 us (5%)
    ppermute x7, waiting for transfers between devices, body(): lax.ppermute(ring[-1], 'dom', [(dev, (dev + 1) % 8) for dev in range(8)])  47.3 us
    psum x1, waiting for transfers between devices, body(): grad_weight, grad_bias = lax.psum((weight_term, bias_term), 'dom')  43.9 us
    reduce_scatter x1, waiting for transfers between devices, body(): lax.psum_scatter(jnp.einsum('ns,sif->nif', select, returned, precision=hi...  39.7 us
    psum x1, waiting for transfers between devices, body(): grad_features = lax.psum(source_part, 'rep')  37 us
    psum x1, waiting for transfers between devices, body(): aggregated = lax.psum(partial_rows, 'rep')  36.3 us
    psum x1, blocking collectives, body(): grad_weight, grad_bias = lax.psum((weight_term, bias_term), 'dom')  13.2 us
  transfers between devices with their start and end apart: 11, of which 11 were waited for; matrix products, arithmetic and copies ran while one was open for 0% of the time, Pallas kernels for 0%

profile of v1, /device:TPU:0, one launch (start us, length us, event | category | flops | bytes accessed | tf_op | source)
XLA Modules:
  0.0 262.7 jit_solution(15597217092499227991)
XLA Ops:
  7.2 0.0 copy-start
  7.2 0.0 copy-start.1
  7.2 0.0 all-reduce.4.cloned.1.call-start
  7.2 0.5 collective-permute-start
  7.7 7.2 %collective-permute-done = f32[256,256]{1,0:T(8,128)S(1)} collective-permute-done((f32[256,256]{1,0:T(8,128)}, f32[256,256]{1,0:T(8,128)S(1)}, u32[]{:S(2)}, u32[]{:S(2)}) %collective-permute-start) | collective-permute-done | bytes 262176 | tf_op jit(solution)/shard_map/ppermute | solution.py:18
  14.9 6.7 %collective-permute-done.1 = f32[256,256]{1,0:T(8,128)S(1)} collective-permute-done((f32[256,256]{1,0:T(8,128)S(1)}, f32[256,256]{1,0:T(8,128)S(1)}, u32[]{:S(2)}, u32[]{:S(2)}) %collective-permute-start.1) | collective-permute-done | bytes 262176 | tf_op jit(solution)/shard_map/ppermute | solution.py:18
  21.6 0.0 collective-permute-start.2
  21.6 6.7 %collective-permute-done.2 = f32[256,256]{1,0:T(8,128)S(1)} collective-permute-done((f32[256,256]{1,0:T(8,128)S(1)}, f32[256,256]{1,0:T(8,128)S(1)}, u32[]{:S(2)}, u32[]{:S(2)}) %collective-permute-start.2) | collective-permute-done | bytes 262176 | tf_op jit(solution)/shard_map/ppermute | solution.py:18
  28.3 0.0 collective-permute-start.3
  28.3 6.7 %collective-permute-done.3 = f32[256,256]{1,0:T(8,128)S(1)} collective-permute-done((f32[256,256]{1,0:T(8,128)S(1)}, f32[256,256]{1,0:T(8,128)S(1)}, u32[]{:S(2)}, u32[]{:S(2)}) %collective-permute-start.3) | collective-permute-done | bytes 262176 | tf_op jit(solution)/shard_map/ppermute | solution.py:18
  35.0 0.0 collective-permute-start.4
  35.0 6.7 %collective-permute-done.4 = f32[256,256]{1,0:T(8,128)S(1)} collective-permute-done((f32[256,256]{1,0:T(8,128)S(1)}, f32[256,256]{1,0:T(8,128)S(1)}, u32[]{:S(2)}, u32[]{:S(2)}) %collective-permute-start.4) | collective-permute-done | bytes 262176 | tf_op jit(solution)/shard_map/ppermute | solution.py:18
  41.7 0.0 collective-permute-start.5
  41.7 6.7 %collective-permute-done.5 = f32[256,256]{1,0:T(8,128)S(1)} collective-permute-done((f32[256,256]{1,0:T(8,128)S(1)}, f32[256,256]{1,0:T(8,128)S(1)}, u32[]{:S(2)}, u32[]{:S(2)}) %collective-permute-start.5) | collective-permute-done | bytes 262176 | tf_op jit(solution)/shard_map/ppermute | solution.py:18
  48.4 0.0 collective-permute-start.6
  48.4 6.7 %collective-permute-done.6 = f32[256,256]{1,0:T(8,128)S(1)} collective-permute-done((f32[256,256]{1,0:T(8,128)S(1)}, f32[256,256]{1,0:T(8,128)S(1)}, u32[]{:S(2)}, u32[]{:S(2)}) %collective-permute-start.6) | collective-permute-done | bytes 262176 | tf_op jit(solution)/shard_map/ppermute | solution.py:18
  55.3 1.0 constant_dynamic-update-slice_fusion.8
  56.2 0.0 copy-start.5
  56.5 0.1 constant_dynamic-slice_fusion
  56.6 0.3 copy-done.5
  56.9 2.3 fusion.8
  59.2 0.0 copy-start.4
  59.2 4.1 %fusion.6 = f32[16,256,128]{2,1,0:T(8,128)} fusion(f32[16,128,256]{2,0,1:T(8,128)S(1)} %fusion.8, bf16[1,16,128,128]{3,2,1,0:T(8,128)(2,1)S(1)} %copy-done), kind=kOutput, calls=%fused_computation.6 | convolution fusion | flops 805306368 | bytes 4718592 | tf_op jit(solution)/shard_map/sij,sjf->sif/dot_general | solution.py:27
  63.3 2.3 copy.15
  65.6 0.8 fusion.2
  66.4 0.7 copy.11
  67.1 0.0 all-reduce.4.cloned.1.call-update
  67.2 0.2 reduce-scatter.2.cloned.1.call-start
  67.4 36.3 %all-reduce.4.cloned.1.call-done = f32[256,256]{1,0:T(8,128)} async-done(((f32[256,256]{1,0:T(8,128)}), f32[256,256]{1,0:T(8,128)}) %all-reduce.4.cloned.1.call-update) | async-done | bytes 262160 | tf_op jit(solution)/shard_map/psum | solution.py:34
  103.7 2.1 fusion.25
  105.8 0.4 fusion.26
  106.3 1.1 fusion.12
  107.4 2.7 %fusion.4 = f32[16,256,128]{2,1,0:T(8,128)S(1)} fusion(f32[16,128,256]{2,0,1:T(8,128)S(1)} %fusion.12, bf16[1,16,128,128]{3,2,1,0:T(8,128)(2,1)S(1)} %copy-done), kind=kOutput, calls=%fused_computation.4 | convolution fusion | flops 805306368 | bytes 4718592 | tf_op jit(solution)/shard_map/sji,sjf->sif/dot_general | solution.py:50
  110.1 2.1 copy.18
  112.2 2.7 %fusion = f32[16,128,256]{2,0,1:T(8,128)S(1)} fusion(f32[16,256,128]{1,0,2:T(8,128)} %copy.18, s32[16]{0:T(128)S(1)} %bitcast.41), kind=kOutput, calls=%fused_computation | convolution fusion | flops 100663552 | bytes 4194368 | tf_op jit(solution)/shard_map/ns,sif->nif/dot_general | solution.py:55
  114.9 2.6 copy.12
  117.5 0.0 reduce-scatter.2.cloned.1.call-update
  117.5 0.0 all-reduce.8.cloned.1.call-start
  117.5 1.3 fusion.27
  118.8 0.0 all-reduce.8.cloned.1.call-update
  118.9 0.0 all-reduce.6.cloned.1.call-start
  118.9 39.7 %reduce-scatter.2.cloned.1.call-done = f32[256,256]{1,0:T(8,128)} async-done(((f32[2048,256]{1,0:T(8,128)}), f32[256,256]{1,0:T(8,128)}) %reduce-scatter.2.cloned.1.call-update) | async-done | bytes 262160 | tf_op jit(solution)/shard_map/reduce_scatter | solution.py:54
  158.6 0.0 all-reduce.6.cloned.1.call-update
  158.6 13.2 %psum.31 = f32[256]{0:T(256)} all-reduce(f32[256]{0:T(256)S(1)} %get-tuple-element.4), channel_id=1, replica_groups=mesh['dom'=8,'rep'=4] {'dom'}, use_global_device_ids=true, to_apply=%region_5.6 | all-reduce | flops 256 | bytes 2048 | tf_op jit(solution)/shard_map/psum | solution.py:47
  171.9 43.9 %all-reduce.8.cloned.1.call-done = f32[256,256]{1,0:T(8,128)} async-done(((f32[256,256]{1,0:T(8,128)}), f32[256,256]{1,0:T(8,128)}) %all-reduce.8.cloned.1.call-update) | async-done | bytes 262160 | tf_op jit(solution)/shard_map/psum | solution.py:47
  215.8 37.0 %all-reduce.6.cloned.1.call-done = f32[256,256]{1,0:T(8,128)} async-done(((f32[256,256]{1,0:T(8,128)}), f32[256,256]{1,0:T(8,128)}) %all-reduce.6.cloned.1.call-update) | async-done | bytes 262160 | tf_op jit(solution)/shard_map/psum | solution.py:62
  252.8 1.7 copy.45
  254.5 1.7 copy.46
  (27 shorter events, 0.3 us)
Async XLA Ops:
  7.2 52.1 %copy-start = (bf16[1,16,128,128]{3,2,1,0:T(8,128)(2,1)S(1)}, bf16[1,16,128,128]{3,2,1,0:T(8,128)(2,1)}, u32[]{:S(2)}) copy-start(bf16[1,16,128,128]{3,2,1,0:T(8,128)(2,1)} %param.8) | copy-start | bytes 1572868
  7.2 49.3 %copy-start.1 = (f32[256,256]{1,0:T(8,128)S(1)}, f32[256,256]{1,0:T(8,128)}, u32[]{:S(2)}) copy-start(f32[256,256]{1,0:T(8,128)} %param.7) | copy-start | bytes 786436
  7.2 96.5 %all-reduce.4.cloned.1.call-start = ((), (), s32[]{:S(2)}) async-start(), calls=%async_computation.1 | async-start | bytes 524288 | tf_op jit(solution)/shard_map/psum | solution.py:34
  7.2 7.7 %collective-permute-start = (f32[256,256]{1,0:T(8,128)}, f32[256,256]{1,0:T(8,128)S(1)}, u32[]{:S(2)}, u32[]{:S(2)}) collective-permute-start(f32[256,256]{1,0:T(8,128)} %param.7), channel_id=1, source_target_pairs={{0,4},{4,8},{8,12},{12,16},{16,20},{20,24},{24,28},{28,0},{1,5},{5... | collective-permute-start | bytes 786440 | tf_op jit(solution)/shard_map/ppermute | solution.py:18
  14.9 6.7 %collective-permute-start.1 = (f32[256,256]{1,0:T(8,128)S(1)}, f32[256,256]{1,0:T(8,128)S(1)}, u32[]{:S(2)}, u32[]{:S(2)}) collective-permute-start(f32[256,256]{1,0:T(8,128)S(1)} %collective-permute-done), channel_id=1, source_target_pairs={{0,4},{4,8},{8,12},{12,16},{16,20},{20,24},{24,28},{28,0},{1,5},{5... | collective-permute-start | bytes 786440 | tf_op jit(solution)/shard_map/ppermute | solution.py:18
  21.6 6.7 %collective-permute-start.2 = (f32[256,256]{1,0:T(8,128)S(1)}, f32[256,256]{1,0:T(8,128)S(1)}, u32[]{:S(2)}, u32[]{:S(2)}) collective-permute-start(f32[256,256]{1,0:T(8,128)S(1)} %collective-permute-done.1), channel_id=1, source_target_pairs={{0,4},{4,8},{8,12},{12,16},{16,20},{20,24},{24,28},{28,0},{1,5},{5... | collective-permute-start | bytes 786440 | tf_op jit(solution)/shard_map/ppermute | solution.py:18
  28.3 6.7 %collective-permute-start.3 = (f32[256,256]{1,0:T(8,128)S(1)}, f32[256,256]{1,0:T(8,128)S(1)}, u32[]{:S(2)}, u32[]{:S(2)}) collective-permute-start(f32[256,256]{1,0:T(8,128)S(1)} %collective-permute-done.2), channel_id=1, source_target_pairs={{0,4},{4,8},{8,12},{12,16},{16,20},{20,24},{24,28},{28,0},{1,5},{5... | collective-permute-start | bytes 786440 | tf_op jit(solution)/shard_map/ppermute | solution.py:18
  35.0 6.7 %collective-permute-start.4 = (f32[256,256]{1,0:T(8,128)S(1)}, f32[256,256]{1,0:T(8,128)S(1)}, u32[]{:S(2)}, u32[]{:S(2)}) collective-permute-start(f32[256,256]{1,0:T(8,128)S(1)} %collective-permute-done.3), channel_id=1, source_target_pairs={{0,4},{4,8},{8,12},{12,16},{16,20},{20,24},{24,28},{28,0},{1,5},{5... | collective-permute-start | bytes 786440 | tf_op jit(solution)/shard_map/ppermute | solution.py:18
  41.7 6.7 %collective-permute-start.5 = (f32[256,256]{1,0:T(8,128)S(1)}, f32[256,256]{1,0:T(8,128)S(1)}, u32[]{:S(2)}, u32[]{:S(2)}) collective-permute-start(f32[256,256]{1,0:T(8,128)S(1)} %collective-permute-done.4), channel_id=1, source_target_pairs={{0,4},{4,8},{8,12},{12,16},{16,20},{20,24},{24,28},{28,0},{1,5},{5... | collective-permute-start | bytes 786440 | tf_op jit(solution)/shard_map/ppermute | solution.py:18
  48.4 6.7 %collective-permute-start.6 = (f32[256,256]{1,0:T(8,128)S(1)}, f32[256,256]{1,0:T(8,128)S(1)}, u32[]{:S(2)}, u32[]{:S(2)}) collective-permute-start(f32[256,256]{1,0:T(8,128)S(1)} %collective-permute-done.5), channel_id=1, source_target_pairs={{0,4},{4,8},{8,12},{12,16},{16,20},{20,24},{24,28},{28,0},{1,5},{5... | collective-permute-start | bytes 786440 | tf_op jit(solution)/shard_map/ppermute | solution.py:18
  56.2 0.7 copy-start.5
  59.2 6.4 %copy-start.4 = (s32[1,16]{1,0:T(1,128)S(1)}, s32[1,16]{1,0:T(1,128)}, u32[]{:S(2)}) copy-start(s32[1,16]{1,0:T(1,128)} %param.9) | copy-start | bytes 196
  63.3 40.4 %copy-start.2 = (f32[256,256]{1,0:T(8,128)S(1)}, f32[256,256]{1,0:T(8,128)}, u32[]{:S(2)}) copy-start(f32[256,256]{1,0:T(8,128)} %param.11) | copy-start | bytes 786436
  63.3 40.4 %copy-start.6 = (f32[256,256]{1,0:T(8,128)S(1)}, f32[256,256]{1,0:T(8,128)}, u32[]{:S(2)}) copy-start(f32[256,256]{1,0:T(8,128)} %param.13) | copy-start | bytes 786436
  63.3 40.4 %copy-start.7 = (f32[256]{0:T(256)S(1)}, f32[256]{0:T(256)}, u32[]{:S(2)}) copy-start(f32[256]{0:T(256)} %param.12) | copy-start | bytes 3076
  67.2 91.5 %reduce-scatter.2.cloned.1.call-start = ((), (), s32[]{:S(2)}) async-start(), calls=%async_computation.2 | async-start | bytes 2359296 | tf_op jit(solution)/shard_map/reduce_scatter | solution.py:54
  114.9 2.6 %copy-start.3 = (f32[256,256]{1,0:T(8,128)S(1)}, f32[256,256]{1,0:T(8,128)}, u32[]{:S(2)}) copy-start(f32[256,256]{1,0:T(8,128)} %all-reduce.4.cloned.1.call-done) | copy-start | bytes 786436
  117.5 98.3 %all-reduce.8.cloned.1.call-start = ((), (), s32[]{:S(2)}) async-start(), calls=%async_computation.4 | async-start | bytes 524288 | tf_op jit(solution)/shard_map/psum | solution.py:47
  118.9 133.9 %all-reduce.6.cloned.1.call-start = ((), (), s32[]{:S(2)}) async-start(), calls=%async_computation.3 | async-start | bytes 524288 | tf_op jit(solution)/shard_map/psum | solution.py:62
Sparse Core Ops, SparseCore 0:
  67.3 36.3 all-reduce.3
  117.6 40.9 reduce-scatter.1
  162.2 53.5 all-reduce.7
  218.1 34.6 all-reduce.5
